TPU v7x, 256 devices: a whole 4x4x8 slice. The times are simulated.
256 devices in a mesh: dp: 64 (over z, y, x_hi), sy: 2 (over x_lo), sx: 2 (over core).
Axes of the slice: x: 4 (x_hi: 2, x_lo: 2; x = x_hi * 2 + x_lo), y: 4, z: 8, core: 2. Of those that a mesh axis runs over, the one named last changes fastest.
Arguments:
- features: bfloat16 [64, 56, 56, 256], P('dp', 'sy', 'sx'), may hold values from -8 to 8
- labels: int32 [64], P('dp'), may hold values from 0 to 999
- grid: int32 [2], replicated, may hold values from 0 to 49
- w_reduce: bfloat16 [3, 256, 64], P(None, None, 'dp'), may hold values from -0.375 to 0.375
- w_spatial: bfloat16 [3, 3, 3, 64, 64], P(None, None, None, None, 'dp'), may hold values from -0.25 to 0.25
- w_expand: bfloat16 [3, 64, 256], P(None, None, 'dp'), may hold values from -0.75 to 0.75
- w_class: bfloat16 [256, 1000], P('dp'), may hold values from -1.5 to 1.5
- dir_reduce: bfloat16 [2, 3, 256, 64], P(None, None, None, 'dp'), may hold values from -6 to 6
- dir_spatial: bfloat16 [2, 3, 3, 3, 64, 64], P(None, None, None, None, None, 'dp'), may hold values from -6 to 6
- dir_expand: bfloat16 [2, 3, 64, 256], P(None, None, None, 'dp'), may hold values from -6 to 6
- dir_class: bfloat16 [2, 256, 1000], P(None, 'dp'), may hold values from -6 to 6
- gain_mid: float32 [3, 2, 64], replicated, may hold values from 0.5 to 1.5
- shift_mid: float32 [3, 2, 64], replicated, may hold values from -3 to 3
- gain_out: float32 [3, 256], replicated, may hold values from 0.5 to 1.5
- shift_out: float32 [3, 256], replicated, may hold values from -3 to 3
Outputs:
- section_out: bfloat16 [64, 56, 56, 256], P('dp', 'sy', 'sx')
- image_loss: float32 [64], P('dp')
- mean_loss: float32 [], replicated
All inputs are finite; a program needn't handle non-finite values.
Results may differ from a plain program's by a relative error of at most 0.012.
Values may be sent and summed in bfloat16 or wider, within the bound.
No kernel may reach another device: no remote copies, remote signals or barrier semaphores. Data moves between devices by JAX's collectives and lax.ppermute only.
A program may use at most 64 MiB of HBM per device.

v0:
```python
import functools

import jax
import jax.numpy as jnp
from jax import lax
from jax.experimental import pallas as pl
from jax.experimental.pallas import tpu as pltpu
from jax.sharding import Mesh
from jax.sharding import PartitionSpec as P

BLOCKS = 3
GRID = 50
EPS_NORM = 1e-06
EPS_BN = 1e-05
FEAT = 256
MID = 64
CLASSES = 1000
TILE = 28
OWN = TILE * TILE
SIDE = 32
CELLS = SIDE * SIDE
OWN_ROWS = TILE * SIDE
HALO = SIDE - TILE
DP = ("z4", "z2", "y", "xh")
GROUP = ("z2", "y", "xh", "sy", "sx")
ALL = ("z4",) + GROUP
TILES = 4
HELD = 4
PAIRS = HELD // 2
IMAGES = 64
CLASS_PART = 16

ROWS = 56
FLAT = 40

PARAMS = pltpu.CompilerParams(vmem_limit_bytes=16 * 1024 * 1024)
VM = pl.BlockSpec(memory_space=pltpu.VMEM)
SM = pl.BlockSpec(memory_space=pltpu.SMEM)


def dot_t(left, right):
    return lax.dot_general(
        left, right, (((1,), (1,)), ((), ())), preferred_element_type=jnp.float32
    )


def tile_moments(y):
    cells = y[:OWN_ROWS].reshape(TILE, SIDE, y.shape[1])
    mean = jnp.sum(jnp.sum(cells, axis=0)[:TILE], axis=0, keepdims=True) * (1.0 / OWN)
    off = cells - mean[None]
    return mean, jnp.sum(jnp.sum(off * off, axis=0)[:TILE], axis=0, keepdims=True)


def halves(pair):
    return [pair[:, :MID], pair[:, MID:]]


def merged(means, squares, cells):
    mean = functools.reduce(jnp.add, means) * (1.0 / len(means))
    total = functools.reduce(jnp.add, squares)
    for m in means:
        total = total + cells * ((m - mean) * (m - mean))
    return mean, total


def received_moments(parts):
    if parts.dtype == jnp.float32:
        return parts
    v = parts.astype(jnp.float32)
    if v.shape[1] == 8:
        return v + pltpu.roll(v, 7, 1) + pltpu.roll(v, 6, 1)
    upper, lower = v[:, :8], v[:, 8:]
    lower = jnp.where(lax.broadcasted_iota(jnp.int32, lower.shape, 1) < 2, lower, 0.0)
    return upper + pltpu.roll(upper, 4, 1) + lower


def normalizer(parts, gain, shift, cells, pairs=False, wide=False):
    parts = received_moments(parts)
    count = parts.shape[0]
    one_row = parts.ndim == 2
    total = jnp.sum(parts, axis=0, keepdims=one_row)
    off = parts - (total * (1.0 / count) if one_row else (total * (1.0 / count))[None])
    spread = jnp.sum(off * off, axis=0, keepdims=one_row)
    if wide:
        flat = lambda v: jnp.concatenate([v[:1], v[1:2]], axis=1)
        mean, squares, spread = flat(total), flat(total[2:4]), flat(spread)
    else:
        mean, squares, spread = total[:1, :MID], total[:1, MID:], spread[:1, :MID]
    mean = mean * (1.0 / count)
    scale = lax.rsqrt((squares + cells * spread) * (1.0 / (cells * count)) + EPS_BN) * gain
    if pairs:
        mean, scale, shift = (jnp.concatenate([v, v], axis=1) for v in (mean, scale, shift))
    return lambda y: (y - mean) * scale + shift


def send(out_ref, row):
    for k in range(out_ref.shape[1]):
        piece = row[:, 128 * k : 128 * (k + 1)].reshape(1, 1, 128)
        out_ref[:, k : k + 1, :] = jnp.broadcast_to(piece, (out_ref.shape[0], 1, 128))


def send_moments(out_ref, tiles, extra=None):
    mean, squares = merged([t[0] for t in tiles], [t[1] for t in tiles], OWN)
    row = jnp.concatenate([mean, squares], axis=1)
    if extra is None:
        return send(out_ref, row)
    rows = [row[:, 128 * k : 128 * (k + 1)] for k in range(row.shape[1] // 128)]
    left = rows[0] if len(rows) == 1 else jnp.concatenate(rows, axis=0)
    pieces = []
    for k in range(3):
        if k == 2:
            left = left[: max(1, len(rows) // 2)]
        piece = left.astype(jnp.bfloat16).astype(jnp.float32)
        pieces.append(piece)
        left = left - piece
    block = jnp.concatenate(pieces + [extra], axis=0).astype(jnp.bfloat16)
    out_ref[...] = jnp.broadcast_to(block[None], (out_ref.shape[0], *block.shape))


def pair_moments(pair):
    mean, squares = tile_moments(pair)
    return list(zip(halves(mean), halves(squares)))


def filters_kernel(
    grid_ref, label_ref, tile_ref, wr_ref, dr_ref, ws_ref, ds_ref, we_ref, de_ref, wc_ref, dc_ref, out_ref, rows, flat, classes, sent
):
    alpha = [(2.0 * grid_ref[k].astype(jnp.float32) + 1.0 - GRID) / GRID for k in range(2)]
    wide = lambda v: v.astype(jnp.float32)

    def filters(base, directions, axes):
        square = lambda v: jnp.sum(v * v, axis=axes, keepdims=True)
        length = jnp.sqrt(square(base))
        value = base
        for k in range(2):
            value = value + alpha[k] * (length / jnp.sqrt(square(directions[k]) + EPS_NORM)) * directions[k]
        return value

    rows[...] = jnp.zeros_like(rows)
    both = wide(dr_ref[...])
    reduce = filters(wide(wr_ref[...]), [both[:, k, :] for k in range(2)], 1)
    for b in range(BLOCKS):
        for q in range(4):
            rows[4 * b + q : 4 * b + q + 1, :] = reduce[b : b + 1, MID * q : MID * (q + 1)]
        both = wide(ds_ref[b])
        spatial = filters(wide(ws_ref[b]), [both[:, :, k, :] for k in range(2)], (0, 1, 2))
        for i in range(3):
            rows[12 + 9 * b + 3 * i : 15 + 9 * b + 3 * i, :] = spatial[i]
        expand = filters(wide(we_ref[b]), [wide(de_ref[k, b]) for k in range(2)], 1)
        for k in range(4):
            rows[FLAT + 3 * k + b : FLAT + 3 * k + b + 1, :] = expand[k : k + 1]
    flat[0:20, :] = jnp.concatenate([rows[pl.ds(h, 20, stride=2), :] for h in range(2)], axis=1)
    tile = tile_ref[0]
    quarter = flat[pl.ds(5 * tile, 5), :]

    classes[...] = jnp.zeros_like(classes)
    classes[0:4, :CLASSES] = wide(wc_ref[...])
    for k in range(2):
        classes[4 + 4 * k : 8 + 4 * k, :CLASSES] = wide(dc_ref[k])
    sent[...] = jnp.zeros_like(sent)
    for b in range(BLOCKS):
        sent[:, MID * b : MID * (b + 1)] = jnp.broadcast_to(rows[pl.ds(FLAT + 3 * tile + b, 1), :], (64, MID))
    for a in range(3):
        row = classes[pl.ds(4 * a + tile, 1), :]
        at = 3 * MID + CLASS_PART * a
        for g in range(64):
            sent[g : g + 1, at : at + CLASS_PART] = row[:, CLASS_PART * g : CLASS_PART * (g + 1)]
    at = 3 * MID + 3 * CLASS_PART
    label = label_ref[0]
    sent[:, at : at + 1] = jnp.full((64, 1), wide(label >> 5), jnp.float32)
    sent[:, at + 1 : at + 2] = jnp.full((64, 1), wide(label & 31), jnp.float32)
    pieces = [sent[:, :128].reshape(64, 1, 128), sent[:, 128:].reshape(64, 1, 128)]
    pieces += [jnp.broadcast_to(quarter[None], (64, 5, 128)), jnp.zeros((64, 1, 128), jnp.float32)]
    copies = jnp.concatenate(pieces, axis=1).astype(jnp.bfloat16)
    for z in range(4):
        out_ref[64 * z : 64 * (z + 1)] = copies


def reduce_kernel(x_ref, w_ref, out_ref):
    send_moments(out_ref, [tile_moments(dot_t(x_ref[...], w_ref[...]))])


def reduced_pair(first, second, w):
    zero = jnp.zeros_like(w)
    return dot_t(first, jnp.concatenate([w, zero], axis=0)) + dot_t(
        second, jnp.concatenate([zero, w], axis=0)
    )


def tile_at(k):
    return slice(CELLS * k, CELLS * (k + 1))


def reduce_of(flat_ref, block):
    return flat_ref[:, FEAT * block : FEAT * (block + 1)]


def spatial_of(flat_ref, block):
    start = FEAT * BLOCKS + 9 * MID * block
    taps = [flat_ref[:, start + MID * t : start + MID * (t + 1)] for t in range(9)]
    zero = jnp.zeros_like(taps[0])
    rows = []
    for i in range(3):
        rows.append(jnp.concatenate([v for t in taps[3 * i : 3 * i + 3] for v in (t, zero)], axis=1))
        rows.append(jnp.concatenate([v for t in taps[3 * i : 3 * i + 3] for v in (zero, t)], axis=1))
    return jnp.concatenate(rows, axis=0)


def expand_of(expand_ref, block):
    w = expand_ref[:, MID * block : MID * (block + 1)]
    zero = jnp.zeros_like(w)
    return [jnp.concatenate(v, axis=1) for v in ((w, zero), (zero, w))]


def convolved(y, norm, inside, taps):
    a = jnp.maximum(norm(y), 0.0) * inside
    sides = [v.astype(jnp.bfloat16) for v in (pltpu.roll(a, 1, 0), a, pltpu.roll(a, CELLS - 1, 0))]
    each = dot_t(jnp.concatenate(sides, axis=1), taps)
    above, here, below = (each[:, 2 * MID * i : 2 * MID * (i + 1)] for i in range(3))
    above = jnp.concatenate([above[CELLS - SIDE :], above[: CELLS - SIDE]], axis=0)
    below = jnp.concatenate([below[SIDE:], below[:SIDE]], axis=0)
    return above + here + below


def first_own_kernel(parts_ref, x_ref, gain_ref, shift_ref, inside_ref, flat_ref, out_ref):
    norm = normalizer(parts_ref[...], gain_ref[...], shift_ref[...], OWN, True)
    y = reduced_pair(x_ref[...], x_ref[...], reduce_of(flat_ref, 0))
    y2 = convolved(y, norm, inside_ref[...], spatial_of(flat_ref, 0))
    send_moments(out_ref, pair_moments(y2)[:1])


def expanded(c, pair_weights, tiles):
    for w in pair_weights:
        tiles.append(tile_moments(dot_t(c[:OWN_ROWS], w)))


def first_expand_kernel(
    span, at_ref, parts_ref, parts2_ref, own_ref, *refs
):
    pieces, (gain_ref, shift_ref, gain2_ref, shift2_ref, inside_ref, flat_ref, expand_ref, extra_ref) = refs[:6], refs[6:14]
    x_ref, c_ref, out_ref = refs[14:]
    half = CELLS // 2
    for off in range(HELD):
        start = lax.rem(at_ref[0] + off, HELD) * CELLS
        for h in range(2):
            piece = own_ref[half * h : half * (h + 1), :] if off == 0 else pieces[2 * (off - 1) + h][...]
            x_ref[pl.ds(pl.multiple_of(start + half * h, half), half), :] = piece
    norm = normalizer(parts_ref[...], gain_ref[...], shift_ref[...], OWN, True)
    norm2 = normalizer(parts2_ref[...], gain2_ref[...], shift2_ref[...], OWN, True)
    taps, weights = spatial_of(flat_ref, 0), expand_of(expand_ref, 0)
    tiles = []
    for p in range(PAIRS):
        y = reduced_pair(x_ref[tile_at(2 * p), :], x_ref[tile_at(2 * p + 1), :], reduce_of(flat_ref, 0))
        y2 = convolved(y, norm, inside_ref[...], taps)
        c = jnp.maximum(norm2(y2), 0.0).astype(jnp.bfloat16)
        c_ref[tile_at(p), :] = c
        expanded(c, weights, tiles)
    send_moments(out_ref, tiles, extra_ref[span[0] : span[1], :])


def spatial_kernel(block, span, parts_ref, y_ref, gain_ref, shift_ref, inside_ref, flat_ref, extra_ref, y2_ref, out_ref):
    norm = normalizer(parts_ref[...], gain_ref[...], shift_ref[...], HELD * OWN, True)
    taps = spatial_of(flat_ref, block)
    tiles = []
    for p in range(PAIRS):
        y2 = convolved(y_ref[tile_at(p), :], norm, inside_ref[...], taps)
        y2_ref[tile_at(p), :] = y2
        tiles += pair_moments(y2)
    send_moments(out_ref, tiles, extra_ref[span[0] : span[1], :])


def expand_kernel(block, span, parts_ref, y_ref, gain_ref, shift_ref, expand_ref, *rest):
    extra = rest[0][span[0] : span[1], :] if span else None
    c_ref, out_ref = rest[-2:]
    norm = normalizer(parts_ref[...], gain_ref[...], shift_ref[...], HELD * OWN, True)
    weights = expand_of(expand_ref, block)
    tiles = []
    for p in range(PAIRS):
        c = jnp.maximum(norm(y_ref[tile_at(p), :]), 0.0).astype(jnp.bfloat16)
        c_ref[tile_at(p), :] = c
        expanded(c, weights, tiles)
    send_moments(out_ref, tiles, extra)


def block_kernel(block, span, parts_ref, c_ref, gain_ref, shift_ref, x_ref, expand_ref, flat_ref, extra_ref, new_ref, y1_ref, out_ref):
    norm = normalizer(parts_ref[...], gain_ref[...], shift_ref[...], HELD * OWN, wide=True)
    weights = expand_of(expand_ref, block)
    tiles = []
    for p in range(PAIRS):
        pair = []
        for h in range(2):
            y = dot_t(c_ref[tile_at(p), :], weights[h])
            x = x_ref[tile_at(2 * p + h), :].astype(jnp.float32)
            new = jnp.maximum(x + norm(y), 0.0).astype(jnp.bfloat16)
            new_ref[tile_at(2 * p + h), :] = new
            pair.append(new)
        y1 = reduced_pair(*pair, reduce_of(flat_ref, block + 1))
        y1_ref[tile_at(p), :] = y1
        tiles += pair_moments(y1)
    send_moments(out_ref, tiles, extra_ref[span[0] : span[1], :])


def last_kernel(block, at_ref, parts_ref, c_ref, gain_ref, shift_ref, x_ref, expand_ref, new_ref, out_ref):
    norm = normalizer(parts_ref[...], gain_ref[...], shift_ref[...], HELD * OWN, wide=True)
    weights = expand_of(expand_ref, block)
    sums = []
    for k in range(HELD):
        c = c_ref[tile_at(k // 2), :][:OWN_ROWS]
        y = dot_t(c, weights[k % 2])
        top = x_ref[tile_at(k), :][:OWN_ROWS].astype(jnp.float32) + norm(y)
        new = jnp.maximum(top, 0.0).astype(jnp.bfloat16)

        @pl.when(at_ref[0] == k)
        def _():
            for row in range(TILE):
                new_ref[row] = new[SIDE * row : SIDE * row + TILE]

        by_col = jnp.sum(new.astype(jnp.float32).reshape(TILE, SIDE, FEAT), axis=0)
        sums.append(jnp.sum(by_col[:TILE], axis=0, keepdims=True))
    send(out_ref, jnp.concatenate(sums, axis=1))


def loss_kernel(mine_ref, pooled_ref, class_ref, tag_ref, own_ref, mean_ref):
    logits = dot_t(pooled_ref[...], class_ref[...])
    classes = lax.broadcasted_iota(jnp.int32, logits.shape, 1)
    summed = jnp.sum(jnp.where(classes < CLASSES, jnp.exp(logits), 0.0), axis=1, keepdims=True)
    picked = jnp.sum(jnp.where(classes == tag_ref[...], logits, 0.0), axis=1, keepdims=True)
    losses = jnp.log(summed) - picked
    image = lax.broadcasted_iota(jnp.int32, losses.shape, 0)
    own_ref[...] = jnp.sum(jnp.where(image == mine_ref[0], losses, 0.0), axis=0, keepdims=True)
    mean_ref[...] = jnp.sum(losses, axis=0, keepdims=True) * (1.0 / IMAGES)


def call(kernel, outs, *args, scratch=(), smem=0, params=PARAMS):
    return pl.pallas_call(
        kernel,
        out_shape=[jax.ShapeDtypeStruct(s, d) for s, d in outs],
        in_specs=[SM] * smem + [VM] * (len(args) - smem),
        out_specs=[VM] * len(outs),
        scratch_shapes=list(scratch),
        compiler_params=params,
    )(*args)


def tile_frame(features, sy, sx):
    own = features[0]
    cols = jnp.where(sx == 0, own[:, TILE - HALO :], own[:, :HALO])
    rows = jnp.where(sy == 0, own[TILE - HALO :], own[:HALO])
    corner = jnp.where(sx == 0, rows[:, TILE - HALO :], rows[:, :HALO])
    cols = lax.ppermute(cols, "sx", [(0, 1), (1, 0)])
    rows = lax.ppermute(rows, "sy", [(0, 1), (1, 0)])
    corner = lax.ppermute(corner, ("sy", "sx"), [(i, 3 - i) for i in range(4)])
    right = jnp.concatenate([cols, corner], axis=0)
    right = jnp.where(sx == 1, jnp.concatenate([right[1:], right[:1]], axis=0), right)
    left = jnp.concatenate([own, rows], axis=0)
    return jnp.concatenate([left, right], axis=1).reshape(CELLS, FEAT)


def inside_image(sy, sx):
    cell = lax.broadcasted_iota(jnp.int32, (CELLS, 2 * MID), 0)
    col = cell % SIDE
    row = ((cell + jnp.where((sx == 1) & (col > TILE), SIDE, 0)) // SIDE) % SIDE
    inside = (row != SIDE - 1 - 3 * sy) & (col != SIDE - 1 - 3 * sx)
    return inside.astype(jnp.float32)


def exchange(copies, axes):
    rows = lax.all_to_all(copies, axes, 0, 0, tiled=True)
    return rows if rows.shape[1] > 1 else rows.reshape(rows.shape[0], -1)


def held_tiles(own, z4):
    fore, back = [(i, (i + 1) % 4) for i in range(4)], [((i + 1) % 4, i) for i in range(4)]
    half = CELLS // 2
    top, bottom = own[:half], own[half:]
    below = [lax.ppermute(v, "z4", fore) for v in (top, bottom)]
    above = [lax.ppermute(v, "z4", back) for v in (bottom, top)]

    def finish(after):
        low, high, after = lax.optimization_barrier((below[0], above[0], after))
        far = [lax.ppermute(low, "z4", fore), lax.ppermute(high, "z4", back)]
        return [above[1], high, *far, low, below[1]], after

    return finish


def per_device(
    features,
    labels,
    grid,
    w_reduce,
    w_spatial,
    w_expand,
    w_class,
    dir_reduce,
    dir_spatial,
    dir_expand,
    dir_class,
    gain_mid,
    shift_mid,
    gain_out,
    shift_out,
):
    z4, sy, sx = (lax.axis_index(a) for a in ("z4", "sy", "sx"))
    tile = 2 * sy + sx
    at = jnp.stack([sy, sx]).astype(jnp.int32)
    with jax.named_scope("filters"):
        (copies,) = call(
            filters_kernel,
            [((256, 8, 128), jnp.bfloat16)],
            grid, labels, tile.astype(jnp.int32).reshape(1),
            w_reduce[:, :, 0], jnp.transpose(dir_reduce[..., 0], (1, 0, 2)),
            w_spatial[..., 0], jnp.transpose(dir_spatial[..., 0], (1, 2, 3, 0, 4)),
            jnp.swapaxes(w_expand, 1, 2), jnp.swapaxes(dir_expand, 2, 3),
            w_class, dir_class,
            scratch=[
                pltpu.VMEM((ROWS, MID), jnp.float32),
                pltpu.VMEM((24, 128), jnp.float32),
                pltpu.VMEM((16, 1024), jnp.float32),
                pltpu.VMEM((64, 256), jnp.float32),
            ],
            smem=3,
            params=pltpu.CompilerParams(),
        )
        small = lax.ppermute(copies[0, 7:], "sx", [(0, 1), (1, 0)])
        features, small = lax.optimization_barrier((features, small))
        at = at + small[0, :2].astype(jnp.int32)
        every = lax.all_to_all(copies, ALL, 0, 0, tiled=True)

    with jax.named_scope("halo"):
        own = tile_frame(features, sy, sx)
        finish = held_tiles(own, z4)

    with jax.named_scope("reduce"):
        first = every.reshape(64, TILES, 8, 128)[:, 0, 2:4, :].reshape(MID, FEAT)
        (sent,) = call(reduce_kernel, [((256, 1, 128), jnp.float32)], own, first)
        later = (every, grid, gain_mid, shift_mid, gain_out, shift_out, at, sent)
        every, point, gain_mid, shift_mid, gain_out, shift_out, at, _ = lax.optimization_barrier(later)
        inside = inside_image(at[0], at[1])
        expand = every[:, :2, :].reshape(256, 256)
        flat = every[:, 2:7, :].reshape(64, FLAT * MID)

    with jax.named_scope("class"):
        rows = expand[:, 3 * MID :]
        high, low = (rows[::TILES, 3 * CLASS_PART + k].astype(jnp.int32) for k in range(2))
        table = high * 32 + low
        tags = table.reshape(4, 16).T.reshape(IMAGES)
        raw = rows[:, : 3 * CLASS_PART].astype(jnp.float32).reshape(FEAT, 3, CLASS_PART)
        norms = jnp.sum(raw * raw, axis=0)
        base = jnp.sqrt(norms[0])
        alpha = (2.0 * point.astype(jnp.float32) + 1.0 - GRID) / GRID
        p_class = raw[:, 0]
        for k in range(2):
            p_class = p_class + alpha[k] * (base / jnp.sqrt(norms[k + 1] + EPS_NORM)) * raw[:, k + 1]
        p_class = p_class.astype(jnp.bfloat16).astype(jnp.float32).T.reshape(2 * CLASS_PART, 128)

    row = lambda v: v.reshape(1, -1)
    mids = [[(row(gain_mid[b, k]), row(shift_mid[b, k])) for k in range(2)] for b in range(BLOCKS)]
    outs = [(row(gain_out[b]), row(shift_out[b])) for b in range(BLOCKS)]
    place = z4.astype(jnp.int32).reshape(1)
    parts = exchange(sent, ALL)
    pieces, after = finish((expand, flat, p_class, tags, inside, mids, outs))
    expand, flat, p_class, tags, inside, mids, outs = after
    mine = HELD * lax.axis_index(("z2", "y", "xh")) + z4
    mine = mine.astype(jnp.int32).reshape(1)
    early = (parts, expand, flat, p_class, tags, inside, mids, outs, place, mine)
    parts, expand, flat, p_class, tags, inside, mids, outs, place, mine = lax.optimization_barrier(early)
    pairs_of = lambda kind: ((PAIRS * CELLS, 2 * MID), kind)
    held = ((HELD * CELLS, FEAT), jnp.bfloat16)
    narrow, wide = ((64, 8, 128), jnp.bfloat16), ((64, 16, 128), jnp.bfloat16)
    spans = [(0, 6), (6, 11), (11, 16), (16, 22), (22, 27), (27, 32)]
    received = []
    for b in range(BLOCKS):
        with jax.named_scope(f"block_{b}"):
            if b == 0:
                (sent,) = call(
                    first_own_kernel, [((256, 1, 128), jnp.float32)],
                    parts, own, *mids[0][0], inside, flat,
                )
                x, c, sent = call(
                    functools.partial(first_expand_kernel, spans.pop(0)), [held, pairs_of(jnp.bfloat16), wide],
                    place, parts, exchange(sent, ALL), own, *pieces, *mids[0][0], *mids[0][1],
                    inside, flat, expand, p_class, smem=1,
                )
                parts = exchange(sent, GROUP)
                received.append((parts, 10))
            else:
                y2, sent = call(
                    functools.partial(spatial_kernel, b, spans.pop(0)), [pairs_of(jnp.float32), narrow],
                    parts, y1, *mids[b][0], inside, flat, p_class,
                )
                parts = exchange(sent, GROUP)
                received.append((parts, 3))
                last = b == BLOCKS - 1
                c, sent = call(
                    functools.partial(expand_kernel, b, None if last else spans.pop(0)),
                    [pairs_of(jnp.bfloat16), ((64, 4, 128), jnp.float32) if last else wide],
                    parts, y2, *mids[b][1], expand, *([] if last else [p_class]),
                )
                parts = exchange(sent, GROUP)
                if not last:
                    received.append((parts, 10))
            args = (parts, c, *outs[b], x, expand)
            if b < BLOCKS - 1:
                x, y1, sent = call(
                    functools.partial(block_kernel, b, spans.pop(0)), [held, pairs_of(jnp.float32), narrow],
                    *args, flat, p_class,
                )
                parts = exchange(sent, GROUP)
                received.append((parts, 3))
            else:
                section, sent = call(
                    functools.partial(last_kernel, b),
                    [((TILE, TILE, FEAT), jnp.bfloat16), ((64, 8, 128), jnp.float32)],
                    place, *args, smem=1,
                )
    with jax.named_scope("loss"):
        pooled = exchange(sent, GROUP).reshape(16, TILES, HELD, FEAT)
        pooled = (jnp.sum(pooled, axis=1) / (OWN * TILES)).astype(jnp.bfloat16).reshape(IMAGES, FEAT)
        arrays, _ = lax.optimization_barrier(([v for v, _ in received], sent))
        arrays = [v[:, start:] for v, (_, start) in zip(arrays, received)]
        classes = jnp.concatenate(arrays, axis=1).reshape(64 * CLASS_PART, FEAT)
        image_loss, mean_loss = call(
            loss_kernel, [((1, 1), jnp.float32)] * 2, mine, pooled, classes, tags.reshape(IMAGES, 1), smem=1
        )
    return section[None], image_loss.reshape(1), mean_loss.reshape(())


def solution(mesh):
    split = Mesh(
        mesh.devices.reshape(4, 2, 4, 2, mesh.shape["sy"], mesh.shape["sx"]), ALL
    )
    tiles = P(DP, "sy", "sx", None)
    return jax.shard_map(
        per_device,
        mesh=split,
        in_specs=(
            tiles,
            P(DP),
            P(),
            P(None, None, DP),
            P(None, None, None, None, DP),
            P(None, None, DP),
            P(DP, None),
            P(None, None, None, DP),
            P(None, None, None, None, None, DP),
            P(None, None, None, DP),
            P(None, DP, None),
            P(),
            P(),
            P(),
            P(),
        ),
        out_specs=(tiles, P(DP), P()),
        check_vma=False,
    )
```

profile of v0, /device:TPU:1, one launch (start us, length us, event | category | flops | bytes accessed | tf_op | source)
XLA Modules:
  0.0 225.1 jit_solution(16651388209811460847)
XLA Ops:
  1.4 2.1 filters.1
  3.5 15.7 %all-to-all-start = ((bf16[256,8,128]{2,1,0:T(8,128)(2,1)}), bf16[256,8,128]{2,1,0:T(8,128)(2,1)S(1)}, u32[]{:S(2)}, u32[]{:S(2)}) async-start(bf16[256,8,128]{2,1,0:T(8,128)(2,1)} %filters.1), calls=%async_computation | async-start | bytes 1048576 | tf_op jit(solution)/shard_map/filters/all_to_all | solution.py:428
  19.8 2.1 collective-permute-start
  23.8 2.0 collective-permute-start.3
  31.3 2.6 %collective-permute-start.6 = (bf16[512,256]{1,0:T(8,128)(2,1)}, bf16[512,256]{1,0:T(8,128)(2,1)S(1)}, u32[]{:S(2)}, u32[]{:S(2)}) collective-permute-start(bf16[512,256]{1,0:T(8,128)(2,1)} %bitcast.15), channel_id=1, source_target_pairs={{64,0},{128,64},{192,128},{0,192},{65,1},{129,65},{193,129},{1,193... | collective-permute-start | bytes 786440 | tf_op jit(solution)/shard_map/halo/ppermute | solution.py:377
  34.0 1.9 collective-permute-start.5
  36.3 2.7 %all-to-all-done = bf16[256,8,128]{2,1,0:T(8,128)(2,1)S(1)} async-done(((bf16[256,8,128]{2,1,0:T(8,128)(2,1)}), bf16[256,8,128]{2,1,0:T(8,128)(2,1)S(1)}, u32[]{:S(2)}, u32[]{:S(2)}) %all-to-all-start) | async-done | bytes 524320 | tf_op jit(solution)/shard_map/filters/all_to_all | solution.py:428
  40.9 10.3 %all-to-all-start.1 = ((f32[256,1,128]{2,1,0:T(1,128)}), f32[256,1,128]{2,1,0:T(1,128)S(1)}, u32[]{:S(2)}, u32[]{:S(2)}) async-start(f32[256,1,128]{2,1,0:T(1,128)} %reduce.4), calls=%async_computation.1 | async-start | bytes 262144 | tf_op jit(solution)/shard_map/all_to_all | solution.py:368
  52.0 1.4 multiply_multiply_fusion.1
  58.8 2.8 %collective-permute-start.7 = (bf16[512,256]{1,0:T(8,128)(2,1)S(1)}, bf16[512,256]{1,0:T(8,128)(2,1)S(1)}, u32[]{:S(2)}, u32[]{:S(2)}) collective-permute-start(bf16[512,256]{1,0:T(8,128)(2,1)S(1)} %collective-permute-done.4.refs_4_), channel_id=1, source_target_pairs={{0,64},{64,128},{128,192},{192,0},{1,65},{65,129},{129,193},{193,1... | collective-permute-start | bytes 786440 | tf_op jit(solution)/shard_map/ppermute | solution.py:381
  61.6 1.3 collective-permute-start.8
  62.9 5.1 %all-to-all-done.1 = f32[256,1,128]{2,1,0:T(1,128)S(1)} async-done(((f32[256,1,128]{2,1,0:T(1,128)}), f32[256,1,128]{2,1,0:T(1,128)S(1)}, u32[]{:S(2)}, u32[]{:S(2)}) %all-to-all-start.1) | async-done | bytes 131104 | tf_op jit(solution)/shard_map/all_to_all | solution.py:368
  68.1 2.1 block_0.3
  70.2 7.7 %all-to-all-start.2 = ((f32[256,1,128]{2,1,0:T(1,128)}), f32[256,1,128]{2,1,0:T(1,128)S(1)}, u32[]{:S(2)}, u32[]{:S(2)}) async-start(f32[256,1,128]{2,1,0:T(1,128)} %block_0.3), calls=%async_computation.2 | async-start | bytes 262144 | tf_op jit(solution)/shard_map/block_0/all_to_all | solution.py:368
  77.9 12.9 %all-to-all-done.2 = f32[256,1,128]{2,1,0:T(1,128)S(1)} async-done(((f32[256,1,128]{2,1,0:T(1,128)}), f32[256,1,128]{2,1,0:T(1,128)S(1)}, u32[]{:S(2)}, u32[]{:S(2)}) %all-to-all-start.2) | async-done | bytes 131104 | tf_op jit(solution)/shard_map/block_0/all_to_all | solution.py:368
  90.8 4.0 %block_0.4 = (bf16[4096,256]{1,0:T(8,128)(2,1)S(1)}, bf16[2048,128]{1,0:T(8,128)(2,1)S(1)}, bf16[64,16,128]{2,1,0:T(8,128)(2,1)S(1)}) custom-call(s32[1]{0:T(128)} %bitcast.43.at_ref, f32[256,128]{1,0:T(8,128)S(1)} %bitcast.116, f32[256,128]{1,0:T(8,128)S(1)} %bitcast.117, bf16[1024,256]{1,0:T(8,128)(2,1)S(1)} %bitcast.105, ...), custom_call_target="tpu_custom_call" | custom-call | tf_op jit(solution)/shard_map/block_0/pallas_call | solution.py:335
  94.7 14.3 %all_to_all.55.parts_ref = bf16[64,16,128]{2,1,0:T(8,128)(2,1)S(1)} all-to-all(bf16[64,16,128]{2,1,0:T(8,128)(2,1)S(1)} %get-tuple-element.134), channel_id=1, replica_groups=mesh['z4'=4,'z2'=2,'y'=4,'xh'=2,'sy'=2,'sx'=2] {'z2','y','xh','sy','sx'}, dimensions={0} | all-to-all | bytes 524288 | tf_op jit(solution)/shard_map/block_0/all_to_all | solution.py:368
  109.1 2.0 block_0.5
  111.1 12.8 %all_to_all.56.parts_ref = bf16[64,8,128]{2,1,0:T(8,128)(2,1)S(1)} all-to-all(bf16[64,8,128]{2,1,0:T(8,128)(2,1)S(1)} %get-tuple-element.139), channel_id=1, replica_groups=mesh['z4'=4,'z2'=2,'y'=4,'xh'=2,'sy'=2,'sx'=2] {'z2','y','xh','sy','sx'}, dimensions={0} | all-to-all | bytes 262144 | tf_op jit(solution)/shard_map/block_0/all_to_all | solution.py:368
  123.9 1.8 block_1.3
  125.7 22.4 %all_to_all.57.parts_ref = bf16[64,8,128]{2,1,0:T(8,128)(2,1)S(1)} all-to-all(bf16[64,8,128]{2,1,0:T(8,128)(2,1)S(1)} %get-tuple-element.143), channel_id=1, replica_groups=mesh['z4'=4,'z2'=2,'y'=4,'xh'=2,'sy'=2,'sx'=2] {'z2','y','xh','sy','sx'}, dimensions={0} | all-to-all | bytes 262144 | tf_op jit(solution)/shard_map/block_1/all_to_all | solution.py:368
  148.0 1.5 block_1.4
  149.6 13.9 %all_to_all.58.parts_ref = bf16[64,16,128]{2,1,0:T(8,128)(2,1)S(1)} all-to-all(bf16[64,16,128]{2,1,0:T(8,128)(2,1)S(1)} %get-tuple-element.147), channel_id=1, replica_groups=mesh['z4'=4,'z2'=2,'y'=4,'xh'=2,'sy'=2,'sx'=2] {'z2','y','xh','sy','sx'}, dimensions={0} | all-to-all | bytes 524288 | tf_op jit(solution)/shard_map/block_1/all_to_all | solution.py:368
  163.4 2.1 block_1.5
  165.5 12.8 %all_to_all.59.parts_ref = bf16[64,8,128]{2,1,0:T(8,128)(2,1)S(1)} all-to-all(bf16[64,8,128]{2,1,0:T(8,128)(2,1)S(1)} %get-tuple-element.152), channel_id=1, replica_groups=mesh['z4'=4,'z2'=2,'y'=4,'xh'=2,'sy'=2,'sx'=2] {'z2','y','xh','sy','sx'}, dimensions={0} | all-to-all | bytes 262144 | tf_op jit(solution)/shard_map/block_1/all_to_all | solution.py:368
  178.3 1.8 block_2.3
  180.0 12.7 %all_to_all.60.parts_ref = bf16[64,8,128]{2,1,0:T(8,128)(2,1)S(1)} all-to-all(bf16[64,8,128]{2,1,0:T(8,128)(2,1)S(1)} %get-tuple-element.156), channel_id=1, replica_groups=mesh['z4'=4,'z2'=2,'y'=4,'xh'=2,'sy'=2,'sx'=2] {'z2','y','xh','sy','sx'}, dimensions={0} | all-to-all | bytes 262144 | tf_op jit(solution)/shard_map/block_2/all_to_all | solution.py:368
  192.7 1.6 block_2.4
  194.3 12.7 %all_to_all.61.parts_ref = f32[64,4,128]{2,1,0:T(4,128)S(1)} all-to-all(f32[64,4,128]{2,1,0:T(4,128)S(1)} %get-tuple-element.160), channel_id=1, replica_groups=mesh['z4'=4,'z2'=2,'y'=4,'xh'=2,'sy'=2,'sx'=2] {'z2','y','xh','sy','sx'}, dimensions={0} | all-to-all | bytes 262144 | tf_op jit(solution)/shard_map/block_2/all_to_all | solution.py:368
  206.9 2.6 %block_2.5 = (bf16[28,28,256]{2,1,0:T(8,128)(2,1)}, f32[64,8,128]{2,1,0:T(8,128)}) custom-call(s32[1]{0:T(128)} %bitcast.43.at_ref, f32[64,4,128]{2,1,0:T(4,128)S(1)} %all_to_all.61.parts_ref, bf16[2048,128]{1,0:T(8,128)(2,1)S(1)} %get-tuple-element.161.c_ref, f32[1,256]{1,0:T(1,128)S(1)} %get-tuple-element.162.gain_ref, ...), custom_call_target="tpu_custom_call" | custom-call | tf_op jit(solution)/shard_map/block_2/pallas_call | solution.py:335
  209.5 4.4 %all-to-all-start.10 = ((f32[64,8,128]{2,1,0:T(8,128)}), f32[64,8,128]{2,1,0:T(8,128)S(1)}, u32[]{:S(2)}, u32[]{:S(2)}) async-start(f32[64,8,128]{2,1,0:T(8,128)} %get-tuple-element.167), calls=%async_computation.10 | async-start | bytes 524288 | tf_op jit(solution)/shard_map/loss/all_to_all | solution.py:368
  215.8 8.0 %all-to-all-done.10 = f32[64,8,128]{2,1,0:T(8,128)S(1)} async-done(((f32[64,8,128]{2,1,0:T(8,128)}), f32[64,8,128]{2,1,0:T(8,128)S(1)}, u32[]{:S(2)}, u32[]{:S(2)}) %all-to-all-start.10) | async-done | bytes 262176 | tf_op jit(solution)/shard_map/loss/all_to_all | solution.py:368
  (79 shorter events, 17.5 us)
Async XLA Ops:
  0.6 28.8 %copy-start = (bf16[1,28,28,256]{3,2,1,0:T(8,128)(2,1)S(1)}, bf16[1,28,28,256]{3,2,1,0:T(8,128)(2,1)}, u32[]{:S(2)}) copy-start(bf16[1,28,28,256]{3,2,1,0:T(8,128)(2,1)} %param.15) | copy-start | bytes 1204228
  3.5 35.5 %all-to-all-start = ((bf16[256,8,128]{2,1,0:T(8,128)(2,1)}), bf16[256,8,128]{2,1,0:T(8,128)(2,1)S(1)}, u32[]{:S(2)}, u32[]{:S(2)}) async-start(bf16[256,8,128]{2,1,0:T(8,128)(2,1)} %filters.1), calls=%async_computation | async-start | bytes 1048576 | tf_op jit(solution)/shard_map/filters/all_to_all | solution.py:428
  19.8 3.0 %collective-permute-start = (bf16[1,128]{1,0:T(2,128)(2,1)S(1)}, bf16[1,128]{1,0:T(2,128)(2,1)S(1)}, u32[]{:S(2)}, u32[]{:S(2)}) collective-permute-start(bf16[1,128]{1,0:T(2,128)(2,1)S(1)} %slice_bitcast_fusion.3), channel_id=1, source_target_pairs={{0,1},{1,0},{2,3},{3,2},{4,5},{5,4},{6,7},{7,6},{8,9},{9,8},{10,11... | collective-permute-start | bytes 776 | tf_op jit(solution)/shard_map/filters/ppermute | solution.py:425
  23.7 5.8 %collective-permute-start.1 = (bf16[4,28,256]{2,1,0:T(8,128)(2,1)S(1)}, bf16[4,28,256]{2,1,0:T(8,128)(2,1)S(1)}, u32[]{:S(2)}, u32[]{:S(2)}) collective-permute-start(bf16[4,28,256]{2,1,0:T(8,128)(2,1)S(1)} %select_bitcast_fusion), channel_id=1, source_target_pairs={{0,2},{2,0},{1,3},{3,1},{4,6},{6,4},{5,7},{7,5},{8,10},{10,8},{9,1... | collective-permute-start | bytes 172040 | tf_op jit(solution)/shard_map/halo/ppermute | solution.py:351
  23.8 5.5 %collective-permute-start.3 = (bf16[4,4,256]{2,1,0:T(4,128)(2,1)S(1)}, bf16[4,4,256]{2,1,0:T(4,128)(2,1)S(1)}, u32[]{:S(2)}, u32[]{:S(2)}) collective-permute-start(bf16[4,4,256]{2,1,0:T(4,128)(2,1)S(1)} %slice_select_fusion.1), channel_id=1, source_target_pairs={{0,3},{1,2},{2,1},{3,0},{4,7},{5,6},{6,5},{7,4},{8,11},{9,10},{10,... | collective-permute-start | bytes 24584 | tf_op jit(solution)/shard_map/halo/ppermute | solution.py:352
  26.8 1.3 collective-permute-start.2
  29.4 21.7 %copy-start.5 = (s32[2]{0:T(128)S(1)}, s32[2]{0:T(128)}, u32[]{:S(2)}) copy-start(s32[2]{0:T(128)} %grid_ref.1) | copy-start | bytes 28
  29.4 22.4 %copy-start.3 = (f32[3,256]{1,0:T(4,128)S(1)}, f32[3,256]{1,0:T(4,128)}, u32[]{:S(2)}) copy-start(f32[3,256]{1,0:T(4,128)} %param.29) | copy-start | bytes 9220
  29.4 22.4 %copy-start.4 = (f32[3,256]{1,0:T(4,128)S(1)}, f32[3,256]{1,0:T(4,128)}, u32[]{:S(2)}) copy-start(f32[3,256]{1,0:T(4,128)} %param.28) | copy-start | bytes 9220
  29.4 22.4 %copy-start.1 = (f32[3,2,64]{2,1,0:T(2,128)S(1)}, f32[3,2,64]{2,1,0:T(2,128)}, u32[]{:S(2)}) copy-start(f32[3,2,64]{2,1,0:T(2,128)} %param.27) | copy-start | bytes 4612
  29.4 22.4 %copy-start.2 = (f32[3,2,64]{2,1,0:T(2,128)S(1)}, f32[3,2,64]{2,1,0:T(2,128)}, u32[]{:S(2)}) copy-start(f32[3,2,64]{2,1,0:T(2,128)} %param.26) | copy-start | bytes 4612
  30.4 27.1 %collective-permute-start.4 = (bf16[512,256]{1,0:T(8,128)(2,1)}, bf16[512,256]{1,0:T(8,128)(2,1)S(1)}, u32[]{:S(2)}, u32[]{:S(2)}) collective-permute-start(bf16[512,256]{1,0:T(8,128)(2,1)} %bitcast.15), channel_id=1, source_target_pairs={{0,64},{64,128},{128,192},{192,0},{1,65},{65,129},{129,193},{193,1... | collective-permute-start | bytes 786440 | tf_op jit(solution)/shard_map/halo/ppermute | solution.py:376
  31.3 46.5 %collective-permute-start.6 = (bf16[512,256]{1,0:T(8,128)(2,1)}, bf16[512,256]{1,0:T(8,128)(2,1)S(1)}, u32[]{:S(2)}, u32[]{:S(2)}) collective-permute-start(bf16[512,256]{1,0:T(8,128)(2,1)} %bitcast.15), channel_id=1, source_target_pairs={{64,0},{128,64},{192,128},{0,192},{65,1},{129,65},{193,129},{1,193... | collective-permute-start | bytes 786440 | tf_op jit(solution)/shard_map/halo/ppermute | solution.py:377
  34.0 24.9 %collective-permute-start.5 = (bf16[512,256]{1,0:T(8,128)(2,1)}, bf16[512,256]{1,0:T(8,128)(2,1)S(1)}, u32[]{:S(2)}, u32[]{:S(2)}) collective-permute-start(bf16[512,256]{1,0:T(8,128)(2,1)} %bitcast.16), channel_id=1, source_target_pairs={{64,0},{128,64},{192,128},{0,192},{65,1},{129,65},{193,129},{1,193... | collective-permute-start | bytes 786440 | tf_op jit(solution)/shard_map/halo/ppermute | solution.py:377
  35.9 41.9 %collective-permute-start.9 = (bf16[512,256]{1,0:T(8,128)(2,1)}, bf16[512,256]{1,0:T(8,128)(2,1)S(1)}, u32[]{:S(2)}, u32[]{:S(2)}) collective-permute-start(bf16[512,256]{1,0:T(8,128)(2,1)} %bitcast.16), channel_id=1, source_target_pairs={{0,64},{64,128},{128,192},{192,0},{1,65},{65,129},{129,193},{193,1... | collective-permute-start | bytes 786440 | tf_op jit(solution)/shard_map/halo/ppermute | solution.py:376
  40.9 27.2 %all-to-all-start.1 = ((f32[256,1,128]{2,1,0:T(1,128)}), f32[256,1,128]{2,1,0:T(1,128)S(1)}, u32[]{:S(2)}, u32[]{:S(2)}) async-start(f32[256,1,128]{2,1,0:T(1,128)} %reduce.4), calls=%async_computation.1 | async-start | bytes 262144 | tf_op jit(solution)/shard_map/all_to_all | solution.py:368
  58.8 19.0 %collective-permute-start.7 = (bf16[512,256]{1,0:T(8,128)(2,1)S(1)}, bf16[512,256]{1,0:T(8,128)(2,1)S(1)}, u32[]{:S(2)}, u32[]{:S(2)}) collective-permute-start(bf16[512,256]{1,0:T(8,128)(2,1)S(1)} %collective-permute-done.4.refs_4_), channel_id=1, source_target_pairs={{0,64},{64,128},{128,192},{192,0},{1,65},{65,129},{129,193},{193,1... | collective-permute-start | bytes 786440 | tf_op jit(solution)/shard_map/ppermute | solution.py:381
  61.6 16.2 %collective-permute-start.8 = (bf16[512,256]{1,0:T(8,128)(2,1)S(1)}, bf16[512,256]{1,0:T(8,128)(2,1)S(1)}, u32[]{:S(2)}, u32[]{:S(2)}) collective-permute-start(bf16[512,256]{1,0:T(8,128)(2,1)S(1)} %collective-permute-done.5.refs_1_), channel_id=1, source_target_pairs={{64,0},{128,64},{192,128},{0,192},{65,1},{129,65},{193,129},{1,193... | collective-permute-start | bytes 786440 | tf_op jit(solution)/shard_map/ppermute | solution.py:381
  70.2 20.6 %all-to-all-start.2 = ((f32[256,1,128]{2,1,0:T(1,128)}), f32[256,1,128]{2,1,0:T(1,128)S(1)}, u32[]{:S(2)}, u32[]{:S(2)}) async-start(f32[256,1,128]{2,1,0:T(1,128)} %block_0.3), calls=%async_computation.2 | async-start | bytes 262144 | tf_op jit(solution)/shard_map/block_0/all_to_all | solution.py:368
  209.5 14.3 %all-to-all-start.10 = ((f32[64,8,128]{2,1,0:T(8,128)}), f32[64,8,128]{2,1,0:T(8,128)S(1)}, u32[]{:S(2)}, u32[]{:S(2)}) async-start(f32[64,8,128]{2,1,0:T(8,128)} %get-tuple-element.167), calls=%async_computation.10 | async-start | bytes 524288 | tf_op jit(solution)/shard_map/loss/all_to_all | solution.py:368
where the time goes:
time: 229 us; the launch traced here: 225 us
  blocking collectives  101 us (44%)
  starting transfers between devices  52.4 us (23%)
  waiting for transfers between devices  33.1 us (14%)
  Pallas kernels  23.5 us (10%)
  local copies, waits for them, and re-layouts  6.06 us (3%)
  other arithmetic  4.69 us (2%)
  between operations  3.91 us (2%)
    all_to_all x7, blocking collectives, exchange(): rows = lax.all_to_all(copies, axes, 0, 0, tiled=True)  101 us
    all_to_all x3, waiting for transfers between devices, exchange(): rows = lax.all_to_all(copies, axes, 0, 0, tiled=True)  26.1 us
    pallas_call x12, Pallas kernels, call(): pl.pallas_call(kernel, out_shape=[jax.ShapeDtypeStruct(s, d) for s, d in...  23.5 us
    all_to_all x3, starting transfers between devices, exchange(): rows = lax.all_to_all(copies, axes, 0, 0, tiled=True)  22.4 us
    all_to_all x1, starting transfers between devices, per_device(): every = lax.all_to_all(copies, ALL, 0, 0, tiled=True)  15.7 us
  transfers between devices with their start and end apart: 14, of which 8 were waited for; matrix products, arithmetic and copies ran while one was open for 5% of the time, Pallas kernels for 1%

commit v1 on v0

--- a/solution.py
+++ b/solution.py
@@ -123,7 +123,7 @@
 
 
 def filters_kernel(
-    grid_ref, label_ref, tile_ref, wr_ref, dr_ref, ws_ref, ds_ref, we_ref, de_ref, wc_ref, dc_ref, out_ref, rows, flat, classes, sent
+    grid_ref, label_ref, tile_ref, wr_ref, dr_ref, ws_ref, ds_ref, we_ref, de_ref, wc_ref, dc_ref, out_ref, small_ref, rows, flat, classes, sent
 ):
     alpha = [(2.0 * grid_ref[k].astype(jnp.float32) + 1.0 - GRID) / GRID for k in range(2)]
     wide = lambda v: v.astype(jnp.float32)
@@ -137,6 +137,7 @@
         return value
 
     rows[...] = jnp.zeros_like(rows)
+    small_ref[...] = jnp.zeros_like(small_ref)
     both = wide(dr_ref[...])
     reduce = filters(wide(wr_ref[...]), [both[:, k, :] for k in range(2)], 1)
     for b in range(BLOCKS):
@@ -405,9 +406,9 @@
     tile = 2 * sy + sx
     at = jnp.stack([sy, sx]).astype(jnp.int32)
     with jax.named_scope("filters"):
-        (copies,) = call(
+        copies, small = call(
             filters_kernel,
-            [((256, 8, 128), jnp.bfloat16)],
+            [((256, 8, 128), jnp.bfloat16), ((1, 128), jnp.float32)],
             grid, labels, tile.astype(jnp.int32).reshape(1),
             w_reduce[:, :, 0], jnp.transpose(dir_reduce[..., 0], (1, 0, 2)),
             w_spatial[..., 0], jnp.transpose(dir_spatial[..., 0], (1, 2, 3, 0, 4)),
@@ -422,7 +423,7 @@
             smem=3,
             params=pltpu.CompilerParams(),
         )
-        small = lax.ppermute(copies[0, 7:], "sx", [(0, 1), (1, 0)])
+        small = lax.ppermute(small, "sx", [(0, 1), (1, 0)])
         features, small = lax.optimization_barrier((features, small))
         at = at + small[0, :2].astype(jnp.int32)
         every = lax.all_to_all(copies, ALL, 0, 0, tiled=True)

time: 229 us -> 228 us (level)
  starting transfers between devices: 52.4 us -> 50.1 us
    all_to_all x1, starting transfers between devices: 15.7 us -> 12.5 us  [per_device(): every = lax.all_to_all(copies, ALL, 0, 0, tiled=True)]
    all_to_all x3, starting transfers between devices: 22.4 us -> 20.1 us  [exchange(): rows = lax.all_to_all(copies, axes, 0, 0, tiled=True)]
  transfers between devices with their start and end apart: 14 -> 14, of which waited for: 8 -> 7; matrix products, arithmetic and copies ran while one was open for 5% -> 4% of each run, Pallas kernels for 1% -> 1%
where the time goes in v1:
time: 228 us; the launch traced here: 223 us
  blocking collectives  101 us (44%)
  starting transfers between devices  50.1 us (22%)
  waiting for transfers between devices  34.5 us (15%)
  Pallas kernels  23.5 us (10%)
  local copies, waits for them, and re-layouts  5.38 us (2%)
  other arithmetic  4.7 us (2%)
  between operations  3.97 us (2%)
    all_to_all x7, blocking collectives, exchange(): rows = lax.all_to_all(copies, axes, 0, 0, tiled=True)  101 us
    all_to_all x3, waiting for transfers between devices, exchange(): rows = lax.all_to_all(copies, axes, 0, 0, tiled=True)  26.3 us
    pallas_call x12, Pallas kernels, call(): pl.pallas_call(kernel, out_shape=[jax.ShapeDtypeStruct(s, d) for s, d in...  23.5 us
    all_to_all x3, starting transfers between devices, exchange(): rows = lax.all_to_all(copies, axes, 0, 0, tiled=True)  20.1 us
    all_to_all x1, starting transfers between devices, per_device(): every = lax.all_to_all(copies, ALL, 0, 0, tiled=True)  12.5 us
    ppermute x2, starting transfers between devices, held_tiles(): above = [lax.ppermute(v, 'z4', back) for v in (bottom, top)]  5 us
    all_to_all x1, waiting for transfers between devices, per_device(): every = lax.all_to_all(copies, ALL, 0, 0, tiled=True)  4.71 us
  transfers between devices with their start and end apart: 14, of which 7 were waited for; matrix products, arithmetic and copies ran while one was open for 4% of the time, Pallas kernels for 1%

profile of v1, /device:TPU:1, one launch (start us, length us, event | category | flops | bytes accessed | tf_op | source)
XLA Modules:
  0.0 223.5 jit_solution(7390564662880446504)
XLA Ops:
  1.4 2.1 filters.1
  3.5 3.2 %collective-permute-start = (f32[1,128]{1,0:T(1,128)}, f32[1,128]{1,0:T(1,128)S(1)}, u32[]{:S(2)}, u32[]{:S(2)}) collective-permute-start(f32[1,128]{1,0:T(1,128)} %get-tuple-element.92), channel_id=1, source_target_pairs={{0,1},{1,0},{2,3},{3,2},{4,5},{5,4},{6,7},{7,6},{8,9},{9,8},{10,11... | collective-permute-start | bytes 1544 | tf_op jit(solution)/shard_map/filters/ppermute | solution.py:426
  6.7 12.5 %all-to-all-start = ((bf16[256,8,128]{2,1,0:T(8,128)(2,1)}), bf16[256,8,128]{2,1,0:T(8,128)(2,1)S(1)}, u32[]{:S(2)}, u32[]{:S(2)}) async-start(bf16[256,8,128]{2,1,0:T(8,128)(2,1)} %get-tuple-element.94), calls=%async_computation | async-start | bytes 1048576 | tf_op jit(solution)/shard_map/filters/all_to_all | solution.py:429
  20.2 1.5 collective-permute-start.1
  21.7 2.5 %collective-permute-start.3 = (bf16[4,4,256]{2,1,0:T(4,128)(2,1)S(1)}, bf16[4,4,256]{2,1,0:T(4,128)(2,1)S(1)}, u32[]{:S(2)}, u32[]{:S(2)}) collective-permute-start(bf16[4,4,256]{2,1,0:T(4,128)(2,1)S(1)} %slice_select_fusion.1), channel_id=1, source_target_pairs={{0,3},{1,2},{2,1},{3,0},{4,7},{5,6},{6,5},{7,4},{8,11},{9,10},{10,... | collective-permute-start | bytes 24584 | tf_op jit(solution)/shard_map/halo/ppermute | solution.py:353
  29.4 2.6 %collective-permute-start.6 = (bf16[512,256]{1,0:T(8,128)(2,1)}, bf16[512,256]{1,0:T(8,128)(2,1)S(1)}, u32[]{:S(2)}, u32[]{:S(2)}) collective-permute-start(bf16[512,256]{1,0:T(8,128)(2,1)} %bitcast.14), channel_id=1, source_target_pairs={{64,0},{128,64},{192,128},{0,192},{65,1},{129,65},{193,129},{1,193... | collective-permute-start | bytes 786440 | tf_op jit(solution)/shard_map/halo/ppermute | solution.py:378
  32.0 2.4 %collective-permute-start.5 = (bf16[512,256]{1,0:T(8,128)(2,1)}, bf16[512,256]{1,0:T(8,128)(2,1)S(1)}, u32[]{:S(2)}, u32[]{:S(2)}) collective-permute-start(bf16[512,256]{1,0:T(8,128)(2,1)} %bitcast.15), channel_id=1, source_target_pairs={{64,0},{128,64},{192,128},{0,192},{65,1},{129,65},{193,129},{1,193... | collective-permute-start | bytes 786440 | tf_op jit(solution)/shard_map/halo/ppermute | solution.py:378
  34.4 4.7 %all-to-all-done = bf16[256,8,128]{2,1,0:T(8,128)(2,1)S(1)} async-done(((bf16[256,8,128]{2,1,0:T(8,128)(2,1)}), bf16[256,8,128]{2,1,0:T(8,128)(2,1)S(1)}, u32[]{:S(2)}, u32[]{:S(2)}) %all-to-all-start) | async-done | bytes 524320 | tf_op jit(solution)/shard_map/filters/all_to_all | solution.py:429
  41.0 8.2 %all-to-all-start.1 = ((f32[256,1,128]{2,1,0:T(1,128)}), f32[256,1,128]{2,1,0:T(1,128)S(1)}, u32[]{:S(2)}, u32[]{:S(2)}) async-start(f32[256,1,128]{2,1,0:T(1,128)} %reduce.4), calls=%async_computation.1 | async-start | bytes 262144 | tf_op jit(solution)/shard_map/all_to_all | solution.py:369
  55.7 1.9 collective-permute-done.5.refs_1_
  57.6 2.5 %collective-permute-start.7 = (bf16[512,256]{1,0:T(8,128)(2,1)S(1)}, bf16[512,256]{1,0:T(8,128)(2,1)S(1)}, u32[]{:S(2)}, u32[]{:S(2)}) collective-permute-start(bf16[512,256]{1,0:T(8,128)(2,1)S(1)} %collective-permute-done.4.refs_4_), channel_id=1, source_target_pairs={{0,64},{64,128},{128,192},{192,0},{1,65},{65,129},{129,193},{193,1... | collective-permute-start | bytes 786440 | tf_op jit(solution)/shard_map/ppermute | solution.py:382
  61.4 5.4 %all-to-all-done.1 = f32[256,1,128]{2,1,0:T(1,128)S(1)} async-done(((f32[256,1,128]{2,1,0:T(1,128)}), f32[256,1,128]{2,1,0:T(1,128)S(1)}, u32[]{:S(2)}, u32[]{:S(2)}) %all-to-all-start.1) | async-done | bytes 131104 | tf_op jit(solution)/shard_map/all_to_all | solution.py:369
  66.8 2.1 block_0.3
  68.9 7.4 %all-to-all-start.2 = ((f32[256,1,128]{2,1,0:T(1,128)}), f32[256,1,128]{2,1,0:T(1,128)S(1)}, u32[]{:S(2)}, u32[]{:S(2)}) async-start(f32[256,1,128]{2,1,0:T(1,128)} %block_0.3), calls=%async_computation.2 | async-start | bytes 262144 | tf_op jit(solution)/shard_map/block_0/all_to_all | solution.py:369
  76.3 12.9 %all-to-all-done.2 = f32[256,1,128]{2,1,0:T(1,128)S(1)} async-done(((f32[256,1,128]{2,1,0:T(1,128)}), f32[256,1,128]{2,1,0:T(1,128)S(1)}, u32[]{:S(2)}, u32[]{:S(2)}) %all-to-all-start.2) | async-done | bytes 131104 | tf_op jit(solution)/shard_map/block_0/all_to_all | solution.py:369
  89.3 4.0 %block_0.4 = (bf16[4096,256]{1,0:T(8,128)(2,1)S(1)}, bf16[2048,128]{1,0:T(8,128)(2,1)S(1)}, bf16[64,16,128]{2,1,0:T(8,128)(2,1)S(1)}) custom-call(s32[1]{0:T(128)} %bitcast.42.at_ref, f32[256,128]{1,0:T(8,128)S(1)} %bitcast.113, f32[256,128]{1,0:T(8,128)S(1)} %bitcast.114, bf16[1024,256]{1,0:T(8,128)(2,1)S(1)} %bitcast.102, ...), custom_call_target="tpu_custom_call" | custom-call | tf_op jit(solution)/shard_map/block_0/pallas_call | solution.py:336
  93.2 14.2 %all_to_all.55.parts_ref = bf16[64,16,128]{2,1,0:T(8,128)(2,1)S(1)} all-to-all(bf16[64,16,128]{2,1,0:T(8,128)(2,1)S(1)} %get-tuple-element.138), channel_id=1, replica_groups=mesh['z4'=4,'z2'=2,'y'=4,'xh'=2,'sy'=2,'sx'=2] {'z2','y','xh','sy','sx'}, dimensions={0} | all-to-all | bytes 524288 | tf_op jit(solution)/shard_map/block_0/all_to_all | solution.py:369
  107.4 2.0 block_0.5
  109.5 12.8 %all_to_all.56.parts_ref = bf16[64,8,128]{2,1,0:T(8,128)(2,1)S(1)} all-to-all(bf16[64,8,128]{2,1,0:T(8,128)(2,1)S(1)} %get-tuple-element.143), channel_id=1, replica_groups=mesh['z4'=4,'z2'=2,'y'=4,'xh'=2,'sy'=2,'sx'=2] {'z2','y','xh','sy','sx'}, dimensions={0} | all-to-all | bytes 262144 | tf_op jit(solution)/shard_map/block_0/all_to_all | solution.py:369
  122.3 1.8 block_1.3
  124.0 22.4 %all_to_all.57.parts_ref = bf16[64,8,128]{2,1,0:T(8,128)(2,1)S(1)} all-to-all(bf16[64,8,128]{2,1,0:T(8,128)(2,1)S(1)} %get-tuple-element.147), channel_id=1, replica_groups=mesh['z4'=4,'z2'=2,'y'=4,'xh'=2,'sy'=2,'sx'=2] {'z2','y','xh','sy','sx'}, dimensions={0} | all-to-all | bytes 262144 | tf_op jit(solution)/shard_map/block_1/all_to_all | solution.py:369
  146.4 1.5 block_1.4
  147.9 13.9 %all_to_all.58.parts_ref = bf16[64,16,128]{2,1,0:T(8,128)(2,1)S(1)} all-to-all(bf16[64,16,128]{2,1,0:T(8,128)(2,1)S(1)} %get-tuple-element.151), channel_id=1, replica_groups=mesh['z4'=4,'z2'=2,'y'=4,'xh'=2,'sy'=2,'sx'=2] {'z2','y','xh','sy','sx'}, dimensions={0} | all-to-all | bytes 524288 | tf_op jit(solution)/shard_map/block_1/all_to_all | solution.py:369
  161.8 2.1 block_1.5
  163.8 12.8 %all_to_all.59.parts_ref = bf16[64,8,128]{2,1,0:T(8,128)(2,1)S(1)} all-to-all(bf16[64,8,128]{2,1,0:T(8,128)(2,1)S(1)} %get-tuple-element.156), channel_id=1, replica_groups=mesh['z4'=4,'z2'=2,'y'=4,'xh'=2,'sy'=2,'sx'=2] {'z2','y','xh','sy','sx'}, dimensions={0} | all-to-all | bytes 262144 | tf_op jit(solution)/shard_map/block_1/all_to_all | solution.py:369
  176.6 1.8 block_2.3
  178.4 12.7 %all_to_all.60.parts_ref = bf16[64,8,128]{2,1,0:T(8,128)(2,1)S(1)} all-to-all(bf16[64,8,128]{2,1,0:T(8,128)(2,1)S(1)} %get-tuple-element.160), channel_id=1, replica_groups=mesh['z4'=4,'z2'=2,'y'=4,'xh'=2,'sy'=2,'sx'=2] {'z2','y','xh','sy','sx'}, dimensions={0} | all-to-all | bytes 262144 | tf_op jit(solution)/shard_map/block_2/all_to_all | solution.py:369
  191.0 1.6 block_2.4
  192.6 12.7 %all_to_all.61.parts_ref = f32[64,4,128]{2,1,0:T(4,128)S(1)} all-to-all(f32[64,4,128]{2,1,0:T(4,128)S(1)} %get-tuple-element.164), channel_id=1, replica_groups=mesh['z4'=4,'z2'=2,'y'=4,'xh'=2,'sy'=2,'sx'=2] {'z2','y','xh','sy','sx'}, dimensions={0} | all-to-all | bytes 262144 | tf_op jit(solution)/shard_map/block_2/all_to_all | solution.py:369
  205.3 2.6 %block_2.5 = (bf16[28,28,256]{2,1,0:T(8,128)(2,1)}, f32[64,8,128]{2,1,0:T(8,128)}) custom-call(s32[1]{0:T(128)} %bitcast.42.at_ref, f32[64,4,128]{2,1,0:T(4,128)S(1)} %all_to_all.61.parts_ref, bf16[2048,128]{1,0:T(8,128)(2,1)S(1)} %get-tuple-element.165.c_ref, f32[1,256]{1,0:T(1,128)S(1)} %get-tuple-element.166.gain_ref, ...), custom_call_target="tpu_custom_call" | custom-call | tf_op jit(solution)/shard_map/block_2/pallas_call | solution.py:336
  207.8 4.4 %all-to-all-start.10 = ((f32[64,8,128]{2,1,0:T(8,128)}), f32[64,8,128]{2,1,0:T(8,128)S(1)}, u32[]{:S(2)}, u32[]{:S(2)}) async-start(f32[64,8,128]{2,1,0:T(8,128)} %get-tuple-element.171), calls=%async_computation.10 | async-start | bytes 524288 | tf_op jit(solution)/shard_map/loss/all_to_all | solution.py:369
  214.1 8.0 %all-to-all-done.10 = f32[64,8,128]{2,1,0:T(8,128)S(1)} async-done(((f32[64,8,128]{2,1,0:T(8,128)}), f32[64,8,128]{2,1,0:T(8,128)S(1)}, u32[]{:S(2)}, u32[]{:S(2)}) %all-to-all-start.10) | async-done | bytes 262176 | tf_op jit(solution)/shard_map/loss/all_to_all | solution.py:369
  (78 shorter events, 16.6 us)
Async XLA Ops:
  0.6 26.5 %copy-start = (bf16[1,28,28,256]{3,2,1,0:T(8,128)(2,1)S(1)}, bf16[1,28,28,256]{3,2,1,0:T(8,128)(2,1)}, u32[]{:S(2)}) copy-start(bf16[1,28,28,256]{3,2,1,0:T(8,128)(2,1)} %param.15) | copy-start | bytes 1204228
  3.5 15.8 %collective-permute-start = (f32[1,128]{1,0:T(1,128)}, f32[1,128]{1,0:T(1,128)S(1)}, u32[]{:S(2)}, u32[]{:S(2)}) collective-permute-start(f32[1,128]{1,0:T(1,128)} %get-tuple-element.92), channel_id=1, source_target_pairs={{0,1},{1,0},{2,3},{3,2},{4,5},{5,4},{6,7},{7,6},{8,9},{9,8},{10,11... | collective-permute-start | bytes 1544 | tf_op jit(solution)/shard_map/filters/ppermute | solution.py:426
  6.7 32.4 %all-to-all-start = ((bf16[256,8,128]{2,1,0:T(8,128)(2,1)}), bf16[256,8,128]{2,1,0:T(8,128)(2,1)S(1)}, u32[]{:S(2)}, u32[]{:S(2)}) async-start(bf16[256,8,128]{2,1,0:T(8,128)(2,1)} %get-tuple-element.94), calls=%async_computation | async-start | bytes 1048576 | tf_op jit(solution)/shard_map/filters/all_to_all | solution.py:429
  20.2 6.9 %collective-permute-start.1 = (bf16[4,28,256]{2,1,0:T(8,128)(2,1)S(1)}, bf16[4,28,256]{2,1,0:T(8,128)(2,1)S(1)}, u32[]{:S(2)}, u32[]{:S(2)}) collective-permute-start(bf16[4,28,256]{2,1,0:T(8,128)(2,1)S(1)} %select_bitcast_fusion), channel_id=1, source_target_pairs={{0,2},{2,0},{1,3},{3,1},{4,6},{6,4},{5,7},{7,5},{8,10},{10,8},{9,1... | collective-permute-start | bytes 172040 | tf_op jit(solution)/shard_map/halo/ppermute | solution.py:352
  21.7 5.2 %collective-permute-start.3 = (bf16[4,4,256]{2,1,0:T(4,128)(2,1)S(1)}, bf16[4,4,256]{2,1,0:T(4,128)(2,1)S(1)}, u32[]{:S(2)}, u32[]{:S(2)}) collective-permute-start(bf16[4,4,256]{2,1,0:T(4,128)(2,1)S(1)} %slice_select_fusion.1), channel_id=1, source_target_pairs={{0,3},{1,2},{2,1},{3,0},{4,7},{5,6},{6,5},{7,4},{8,11},{9,10},{10,... | collective-permute-start | bytes 24584 | tf_op jit(solution)/shard_map/halo/ppermute | solution.py:353
  25.1 1.3 collective-permute-start.2
  27.0 22.2 %copy-start.5 = (s32[2]{0:T(128)S(1)}, s32[2]{0:T(128)}, u32[]{:S(2)}) copy-start(s32[2]{0:T(128)} %grid_ref.1) | copy-start | bytes 28
  27.0 22.9 %copy-start.3 = (f32[3,256]{1,0:T(4,128)S(1)}, f32[3,256]{1,0:T(4,128)}, u32[]{:S(2)}) copy-start(f32[3,256]{1,0:T(4,128)} %param.29) | copy-start | bytes 9220
  27.1 22.9 %copy-start.4 = (f32[3,256]{1,0:T(4,128)S(1)}, f32[3,256]{1,0:T(4,128)}, u32[]{:S(2)}) copy-start(f32[3,256]{1,0:T(4,128)} %param.28) | copy-start | bytes 9220
  27.1 22.9 %copy-start.1 = (f32[3,2,64]{2,1,0:T(2,128)S(1)}, f32[3,2,64]{2,1,0:T(2,128)}, u32[]{:S(2)}) copy-start(f32[3,2,64]{2,1,0:T(2,128)} %param.27) | copy-start | bytes 4612
  27.1 22.9 %copy-start.2 = (f32[3,2,64]{2,1,0:T(2,128)S(1)}, f32[3,2,64]{2,1,0:T(2,128)}, u32[]{:S(2)}) copy-start(f32[3,2,64]{2,1,0:T(2,128)} %param.26) | copy-start | bytes 4612
  28.0 27.6 %collective-permute-start.4 = (bf16[512,256]{1,0:T(8,128)(2,1)}, bf16[512,256]{1,0:T(8,128)(2,1)S(1)}, u32[]{:S(2)}, u32[]{:S(2)}) collective-permute-start(bf16[512,256]{1,0:T(8,128)(2,1)} %bitcast.14), channel_id=1, source_target_pairs={{0,64},{64,128},{128,192},{192,0},{1,65},{65,129},{129,193},{193,1... | collective-permute-start | bytes 786440 | tf_op jit(solution)/shard_map/halo/ppermute | solution.py:377
  29.4 46.9 %collective-permute-start.6 = (bf16[512,256]{1,0:T(8,128)(2,1)}, bf16[512,256]{1,0:T(8,128)(2,1)S(1)}, u32[]{:S(2)}, u32[]{:S(2)}) collective-permute-start(bf16[512,256]{1,0:T(8,128)(2,1)} %bitcast.14), channel_id=1, source_target_pairs={{64,0},{128,64},{192,128},{0,192},{65,1},{129,65},{193,129},{1,193... | collective-permute-start | bytes 786440 | tf_op jit(solution)/shard_map/halo/ppermute | solution.py:378
  32.0 25.5 %collective-permute-start.5 = (bf16[512,256]{1,0:T(8,128)(2,1)}, bf16[512,256]{1,0:T(8,128)(2,1)S(1)}, u32[]{:S(2)}, u32[]{:S(2)}) collective-permute-start(bf16[512,256]{1,0:T(8,128)(2,1)} %bitcast.15), channel_id=1, source_target_pairs={{64,0},{128,64},{192,128},{0,192},{65,1},{129,65},{193,129},{1,193... | collective-permute-start | bytes 786440 | tf_op jit(solution)/shard_map/halo/ppermute | solution.py:378
  34.4 41.9 %collective-permute-start.9 = (bf16[512,256]{1,0:T(8,128)(2,1)}, bf16[512,256]{1,0:T(8,128)(2,1)S(1)}, u32[]{:S(2)}, u32[]{:S(2)}) collective-permute-start(bf16[512,256]{1,0:T(8,128)(2,1)} %bitcast.15), channel_id=1, source_target_pairs={{0,64},{64,128},{128,192},{192,0},{1,65},{65,129},{129,193},{193,1... | collective-permute-start | bytes 786440 | tf_op jit(solution)/shard_map/halo/ppermute | solution.py:377
  41.0 25.8 %all-to-all-start.1 = ((f32[256,1,128]{2,1,0:T(1,128)}), f32[256,1,128]{2,1,0:T(1,128)S(1)}, u32[]{:S(2)}, u32[]{:S(2)}) async-start(f32[256,1,128]{2,1,0:T(1,128)} %reduce.4), calls=%async_computation.1 | async-start | bytes 262144 | tf_op jit(solution)/shard_map/all_to_all | solution.py:369
  57.6 18.7 %collective-permute-start.7 = (bf16[512,256]{1,0:T(8,128)(2,1)S(1)}, bf16[512,256]{1,0:T(8,128)(2,1)S(1)}, u32[]{:S(2)}, u32[]{:S(2)}) collective-permute-start(bf16[512,256]{1,0:T(8,128)(2,1)S(1)} %collective-permute-done.4.refs_4_), channel_id=1, source_target_pairs={{0,64},{64,128},{128,192},{192,0},{1,65},{65,129},{129,193},{193,1... | collective-permute-start | bytes 786440 | tf_op jit(solution)/shard_map/ppermute | solution.py:382
  60.1 16.2 %collective-permute-start.8 = (bf16[512,256]{1,0:T(8,128)(2,1)S(1)}, bf16[512,256]{1,0:T(8,128)(2,1)S(1)}, u32[]{:S(2)}, u32[]{:S(2)}) collective-permute-start(bf16[512,256]{1,0:T(8,128)(2,1)S(1)} %collective-permute-done.5.refs_1_), channel_id=1, source_target_pairs={{64,0},{128,64},{192,128},{0,192},{65,1},{129,65},{193,129},{1,193... | collective-permute-start | bytes 786440 | tf_op jit(solution)/shard_map/ppermute | solution.py:382
  68.9 20.4 %all-to-all-start.2 = ((f32[256,1,128]{2,1,0:T(1,128)}), f32[256,1,128]{2,1,0:T(1,128)S(1)}, u32[]{:S(2)}, u32[]{:S(2)}) async-start(f32[256,1,128]{2,1,0:T(1,128)} %block_0.3), calls=%async_computation.2 | async-start | bytes 262144 | tf_op jit(solution)/shard_map/block_0/all_to_all | solution.py:369
  207.8 14.3 %all-to-all-start.10 = ((f32[64,8,128]{2,1,0:T(8,128)}), f32[64,8,128]{2,1,0:T(8,128)S(1)}, u32[]{:S(2)}, u32[]{:S(2)}) async-start(f32[64,8,128]{2,1,0:T(8,128)} %get-tuple-element.171), calls=%async_computation.10 | async-start | bytes 524288 | tf_op jit(solution)/shard_map/loss/all_to_all | solution.py:369
